TPU v7x, 32 devices: a whole 2x2x4 slice. The times are simulated.
32 devices in a mesh: seq: 4 (over z), exp: 8 (over y, x, core).
Axes of the slice: x: 2, y: 2, z: 4, core: 2. Of those that a mesh axis runs over, the one named last changes fastest.
Arguments:
- queries: bfloat16 [32, 4096], P('exp'), may hold values from -80 to 80
- new_kv: bfloat16 [2, 32, 512], P(None, 'exp'), may hold values from -4 to 4
- kv_cache: bfloat16 [2, 32, 2048, 512], P(None, 'exp', 'seq'), may hold values from -4 to 4
- lengths: int32 [32], P('exp'), may hold values from 1 to 2048, as said below
- out_proj: bfloat16 [4096, 2048], P('seq'), may hold values from -0.09375 to 0.09375
- hidden_in: float32 [32, 2048], P('exp'), may hold values from -6 to 6
- norm_gain: float32 [2048], replicated, may hold values from 0.1 to 1.9
- router: bfloat16 [2048, 32], replicated, may hold values from -0.125 to 0.125
- expert_ids: int32 [32, 8], replicated, may hold values from 0 to 31, all different within a row; in each aligned block of 32 rows (0 to 31, 32 to 63, ...) at most 16 rows name the same one
- w_gate_up: bfloat16 [32, 2048, 1536], P(('seq', 'exp')), may hold values from -0.125 to 0.125
- w_down: bfloat16 [32, 768, 2048], P(('seq', 'exp')), may hold values from -0.21875 to 0.21875
- talk_proj: bfloat16 [2048, 1024], replicated, may hold values from -0.125 to 0.125
- talk_gain: float32 [1024], replicated, may hold values from 0.1 to 1.9
- talk_router: bfloat16 [1024, 32], replicated, may hold values from -0.1875 to 0.1875
- talk_ids: int32 [32, 8], replicated, may hold values from 0 to 31, all different within a row; in each aligned block of 32 rows (0 to 31, 32 to 63, ...) at most 16 rows name the same one
- talk_gate_up: bfloat16 [32, 1024, 768], P(('seq', 'exp')), may hold values from -0.1875 to 0.1875
- talk_down: bfloat16 [32, 384, 1024], P(('seq', 'exp')), may hold values from -0.3125 to 0.3125
Outputs:
- thinker_out: float32 [32, 2048], P('exp')
- talker_out: float32 [32, 1024], P('exp')
Inputs may be any that keep to these rules, and one draw needn't show every extreme that they name: `lengths`: some conversation uses all 2048 positions and some uses only one. `expert_ids`: each row names 8 different experts. Over all 32 rows no expert is named more than 16 times, and in every draw some expert is named exactly 16 times. `talk_ids`: as for expert_ids.
All inputs are finite; a program needn't handle non-finite values.
Results may differ from a plain program's by a relative error of at most 0.011.
Values may be sent and summed in bfloat16 or wider, within the bound.
A program may use at most 128 MiB of HBM per device.

v0:
```python
import jax
import jax.numpy as jnp
from jax import lax
from jax.sharding import PartitionSpec as P

H = 32
KVH = 4
HD = 128


def joined(shard, axis, combine):
    everything = jax.tree.map(lambda part: lax.all_gather(part, axis), shard)
    first = jax.tree.map(lambda part: part[0], everything)

    def turn(k, so_far):
        return combine(so_far, jax.tree.map(lambda part: part[k], everything))

    return lax.fori_loop(1, lax.axis_size(axis), turn, first)


def merge_pair(former, latter):
    peak_a, total_a, mixed_a = former
    peak_b, total_b, mixed_b = latter
    peak = jnp.maximum(peak_a, peak_b)
    scale_a = jnp.exp(peak_a - peak)
    scale_b = jnp.exp(peak_b - peak)
    return (
        peak,
        total_a * scale_a + total_b * scale_b,
        mixed_a * scale_a[..., None] + mixed_b * scale_b[..., None],
    )


def expert_layer(stream, gain, router_w, picks, gate_up, down_w):
    own_rows, width = stream.shape
    all_rows, top_count = picks.shape
    experts = router_w.shape[1]
    local_experts = gate_up.shape[0]
    inner_width = down_w.shape[1]
    capacity = max(2, 2 * all_rows * top_count // experts)
    normed = (
        stream * lax.rsqrt(jnp.mean(stream * stream, axis=1, keepdims=True) + 1e-06) * gain
    ).astype(jnp.bfloat16)
    first_expert = (
        lax.axis_index("seq") * lax.axis_size("exp") + lax.axis_index("exp")
    ) * local_experts
    mine = first_expert + jnp.arange(local_experts, dtype=jnp.int32)
    flat_ids = picks.reshape(-1)
    match = (flat_ids[:, None] == mine[None, :]).astype(jnp.int32)
    rank = jnp.cumsum(match, axis=0) - 1
    slot_marks = jnp.logical_and(
        rank[:, :, None] == jnp.arange(capacity, dtype=jnp.int32)[None, None, :],
        match[:, :, None] == 1,
    ).astype(jnp.float32)
    placing = jnp.sum(slot_marks.reshape(all_rows, top_count, local_experts, capacity), axis=1)
    placing_bf = placing.astype(jnp.bfloat16)
    block = placing_bf
    slot_rows = jnp.einsum(
        "rec,rw->ecw",
        block,
        lax.all_gather(normed, "exp", axis=0, tiled=True),
        preferred_element_type=jnp.float32,
    ).astype(jnp.bfloat16)
    logits = jnp.einsum("ecw,wx->ecx", slot_rows, router_w, preferred_element_type=jnp.float32)
    labels = jnp.arange(experts, dtype=jnp.int32)
    pick_marks = (picks[:, :, None] == labels[None, None, :]).astype(jnp.float32)
    slot_picks = jnp.einsum("rec,rkx->eckx", placing, pick_marks, precision=lax.Precision.HIGHEST)
    picked = jnp.sum(slot_picks * logits[:, :, None, :], axis=-1)
    sigmoid_total = jnp.sum(jax.nn.sigmoid(picked), axis=-1)
    own_marks = (labels[None, :] == mine[:, None]).astype(jnp.float32)
    own_logit = jnp.sum(logits * own_marks[:, None, :], axis=-1)
    gates = jax.nn.sigmoid(own_logit) / sigmoid_total
    both = jnp.einsum("ecw,ewf->ecf", slot_rows, gate_up, preferred_element_type=jnp.float32)
    inner = (jax.nn.silu(both[..., :inner_width]) * both[..., inner_width:]).astype(jnp.bfloat16)
    replies = jnp.einsum("ecf,efw->ecw", inner, down_w, preferred_element_type=jnp.float32).astype(
        jnp.bfloat16
    )
    weighted = gates[:, :, None] * replies.astype(jnp.float32)
    block = placing
    summed = lax.psum(
        jnp.einsum("rec,ecw->rw", block, weighted, precision=lax.Precision.HIGHEST), ("seq", "exp")
    )
    gathered = lax.dynamic_slice_in_dim(summed, lax.axis_index("exp") * own_rows, own_rows, 0)
    return stream + gathered


def local_attention(queries, new_kv, kv_cache, lengths):
    count = queries.shape[0]
    span = kv_cache.shape[2]
    groups = H // KVH
    scale = HD ** (-0.5)
    query_b = queries.reshape(count, KVH, groups, HD)
    keys = kv_cache[0].reshape(count, span, KVH, HD)
    values = kv_cache[1].reshape(count, span, KVH, HD)
    fresh_keys = new_kv[0].reshape(count, KVH, HD)
    fresh_values = new_kv[1].reshape(count, KVH, HD)
    cached = (
        jnp.einsum("ckjd,cpkd->ckjp", query_b, keys, preferred_element_type=jnp.float32) * scale
    )
    fresh = (
        jnp.einsum("ckjd,ckd->ckj", query_b, fresh_keys, preferred_element_type=jnp.float32) * scale
    )
    seq_index = lax.axis_index("seq")
    places = seq_index * span + jnp.arange(span, dtype=jnp.int32)
    valid = places[None, :] < lengths[:, None]
    owner = seq_index == 0
    masked = jnp.where(valid[:, None, None, :], cached, -1e30)
    fresh_masked = jnp.where(owner, fresh, -1e30)
    peak = jnp.maximum(jnp.max(masked, axis=-1), fresh_masked)
    weights = jnp.where(valid[:, None, None, :], jnp.exp(masked - peak[..., None]), 0.0)
    fresh_weight = jnp.where(owner, jnp.exp(fresh_masked - peak), 0.0)
    totals = jnp.sum(weights, axis=-1) + fresh_weight
    upper = weights.astype(jnp.bfloat16)
    lower = (weights - upper.astype(jnp.float32)).astype(jnp.bfloat16)
    mixed = jnp.einsum("ckjp,cpkd->ckjd", upper, values, preferred_element_type=jnp.float32)
    mixed = mixed + jnp.einsum("ckjp,cpkd->ckjd", lower, values, preferred_element_type=jnp.float32)
    mixed = mixed + fresh_weight[..., None] * fresh_values[:, :, None, :].astype(jnp.float32)
    return (peak.reshape(count, H), totals.reshape(count, H), mixed.reshape(count, H, HD))


def on_device(
    queries,
    new_kv,
    kv_cache,
    lengths,
    out_proj,
    hidden_in,
    norm_gain,
    router,
    expert_ids,
    w_gate_up,
    w_down,
    talk_proj,
    talk_gain,
    talk_router,
    talk_ids,
    talk_gate_up,
    talk_down,
):
    count = queries.shape[0]
    seq_ways = lax.axis_size("seq")
    own_heads = H // seq_ways
    peak, totals, mixed = local_attention(queries, new_kv, kv_cache, lengths)
    peak, totals, mixed = joined((peak, totals, mixed), "seq", merge_pair)
    first_head = lax.axis_index("seq") * own_heads
    totals = lax.dynamic_slice_in_dim(totals, first_head, own_heads, 1)
    mixed = lax.dynamic_slice_in_dim(mixed, first_head, own_heads, 1)
    attn = (mixed / totals[..., None]).reshape(count, own_heads * HD).astype(jnp.bfloat16)
    head_term = jnp.dot(attn, out_proj, preferred_element_type=jnp.float32)
    projected = lax.psum(head_term, "seq")
    state = hidden_in + projected
    thinker = expert_layer(state, norm_gain, router, expert_ids, w_gate_up, w_down)
    talk_in = jnp.dot(thinker.astype(jnp.bfloat16), talk_proj, preferred_element_type=jnp.float32)
    talker = expert_layer(talk_in, talk_gain, talk_router, talk_ids, talk_gate_up, talk_down)
    return (thinker, talker)


def solution(mesh):
    placed = (
        P("exp", None),
        P(None, "exp", None),
        P(None, "exp", "seq", None),
        P("exp"),
        P("seq", None),
        P("exp", None),
        P(),
        P(),
        P(),
        P(("seq", "exp"), None, None),
        P(("seq", "exp"), None, None),
        P(),
        P(),
        P(),
        P(),
        P(("seq", "exp"), None, None),
        P(("seq", "exp"), None, None),
    )
    return jax.shard_map(
        on_device,
        mesh=mesh,
        in_specs=placed,
        out_specs=(P("exp", None), P("exp", None)),
        check_vma=False,
    )
```

profile of v0, /device:TPU:0, one launch (start us, length us, event | category | flops | bytes accessed | tf_op | source)
XLA Modules:
  0.0 377.7 jit_solution(14250059831365037790)
XLA Ops:
  7.2 1.4 broadcast_compare_fusion.1
  8.7 0.1 reshape.478
  8.8 0.3 reduce-window.14
  9.2 0.7 slice_reduce_fusion.1
  9.9 0.5 compare_convert_fusion.2
  10.5 4.4 %fusion.76 = (bf16[1,4,512,512]{3,2,1,0:T(8,128)(2,1)}, bf16[1,4,512,512]{3,2,1,0:T(8,128)(2,1)}) fusion(bf16[2,4,512,512]{3,2,1,0:T(8,128)(2,1)} %param.21), kind=kLoop, calls=%fused_computation.119 | loop fusion | bytes 8388608 | tf_op jit(solution)/shard_map/slice | solution.py:94
  14.9 4.2 %copy.66 = bf16[1,4,512,512]{2,3,1,0:T(8,128)(2,1)} copy(bf16[1,4,512,512]{3,2,1,0:T(8,128)(2,1)} %get-tuple-element.208) | data formatting | bytes 4194304
  19.2 0.1 fusion.47
  19.3 2.1 fusion.77
  21.4 0.1 all_gather_reshape.9
  21.5 13.5 %all_gather.15 = f32[4,4,32]{2,1,0:T(4,128)S(1)} all-gather(f32[1,4,32]{2,1,0:T(4,128)S(1)} %all_gather_reshape.9), channel_id=1, replica_groups=mesh['seq'=4,'exp'=8] {'seq'}, dimensions={0}, use_global_device_ids=true | all-gather | bytes 2560 | tf_op jit(solution)/shard_map/all_gather | solution.py:12
  35.0 0.2 fusion.33
  35.3 11.9 %all_gather.16 = f32[4,4,32]{2,1,0:T(4,128)S(1)} all-gather(f32[1,4,32]{2,1,0:T(4,128)S(1)} %all_gather_reshape.10), channel_id=1, replica_groups=mesh['seq'=4,'exp'=8] {'seq'}, dimensions={0}, use_global_device_ids=true | all-gather | bytes 2560 | tf_op jit(solution)/shard_map/all_gather | solution.py:12
  47.2 4.2 %copy.67 = bf16[1,4,512,512]{2,3,1,0:T(8,128)(2,1)} copy(bf16[1,4,512,512]{3,2,1,0:T(8,128)(2,1)} %get-tuple-element.207) | data formatting | bytes 4194304
  51.4 2.3 fusion.34
  53.7 2.3 fusion.23
  55.9 13.8 %all_gather.17 = f32[4,4,32,128]{3,2,1,0:T(8,128)S(1)} all-gather(f32[1,4,32,128]{3,2,1,0:T(8,128)S(1)} %fusion.23), channel_id=1, replica_groups=mesh['seq'=4,'exp'=8] {'seq'}, dimensions={0}, use_global_device_ids=true | all-gather | bytes 327680 | tf_op jit(solution)/shard_map/all_gather | solution.py:12
  69.8 0.5 while.19
  69.8 0.1 fusion.101
  69.9 0.1 fusion.101
  70.1 0.1 fusion.101
  70.5 2.9 fusion.61
  73.3 17.0 %psum.21 = f32[4,2048]{1,0:T(4,128)S(1)} all-reduce(f32[4,2048]{1,0:T(4,128)S(1)} %fusion.61), channel_id=1, replica_groups=mesh['seq'=4,'exp'=8] {'seq'}, use_global_device_ids=true, to_apply=%region_4.5 | all-reduce | flops 8192 | bytes 65536 | tf_op jit(solution)/shard_map/psum | solution.py:150
  90.3 0.2 reduce-window.15
  90.7 0.1 multiply_reduce_fusion
  90.9 9.2 %all-gather = bf16[8,4,2048]{2,1,0:T(4,128)(2,1)S(1)} all-gather(bf16[1,4,2048]{2,1,0:T(4,128)(2,1)S(1)} %fusion.55), channel_id=1, replica_groups=mesh['seq'=4,'exp'=8] {'exp'}, dimensions={0}, use_global_device_ids=true | all-gather | bytes 147456 | tf_op jit(solution)/shard_map/all_gather | solution.py:61
  100.2 0.1 convolution_convert_fusion
  100.4 1.2 multiply_reduce_fusion.3
  101.6 0.3 fusion.29
  101.9 3.7 fusion.7
  105.7 0.5 fusion.16
  106.2 1.1 fusion.78
  107.5 0.1 reshape.479
  107.6 0.3 reduce-window.16
  108.0 0.2 slice_reduce_fusion
  108.2 0.2 reduce-window.19
  108.6 121.4 %all-reduce.3.cloned.1.call-done = f32[32,2048]{1,0:T(8,128)} async-done(((f32[32,2048]{1,0:T(8,128)}), f32[32,2048]{1,0:T(8,128)}) %all-reduce.3.cloned.1.call-update) | async-done | bytes 262160 | tf_op jit(solution)/shard_map/psum | solution.py:80
  230.0 0.8 dynamic-slice_add_fusion
  230.9 3.0 multiply_reduce_fusion.1
  234.0 9.2 %all-gather.1 = bf16[8,4,1024]{2,1,0:T(4,128)(2,1)S(1)} all-gather(bf16[1,4,1024]{2,1,0:T(4,128)(2,1)S(1)} %fusion.60), channel_id=1, replica_groups=mesh['seq'=4,'exp'=8] {'exp'}, dimensions={0}, use_global_device_ids=true | all-gather | bytes 73728 | tf_op jit(solution)/shard_map/all_gather | solution.py:61
  243.2 0.1 convolution_convert_fusion.2
  243.3 0.2 multiply_reduce_fusion.2
  243.5 0.3 fusion.30
  243.9 1.7 fusion.24
  245.6 1.4 fusion.28
  247.0 1.0 fusion.79
  248.0 121.5 %all-reduce.5.cloned.1.call-done = f32[32,1024]{1,0:T(8,128)} async-done(((f32[32,1024]{1,0:T(8,128)}), f32[32,1024]{1,0:T(8,128)}) %all-reduce.5.cloned.1.call-update) | async-done | bytes 131088 | tf_op jit(solution)/shard_map/psum | solution.py:80
  369.5 1.4 dynamic-slice_add_fusion.1
  (76 shorter events, 1.8 us)
Async XLA Ops:
  7.2 98.5 %copy-start = (bf16[1,768,2048]{2,1,0:T(8,128)(2,1)S(1)}, bf16[1,768,2048]{2,1,0:T(8,128)(2,1)}, u32[]{:S(2)}) copy-start(bf16[1,768,2048]{2,1,0:T(8,128)(2,1)} %param.29) | copy-start | bytes 9437188
  7.2 222.8 %all-reduce.3.cloned.1.call-start = ((), (), s32[]{:S(2)}) async-start(), calls=%async_computation | async-start | bytes 524288 | tf_op jit(solution)/shard_map/psum | solution.py:80
  14.9 4.2 %copy-start.6 = (bf16[2,4,512]{2,1,0:T(4,128)(2,1)S(1)}, bf16[2,4,512]{2,1,0:T(4,128)(2,1)}, u32[]{:S(2)}) copy-start(bf16[2,4,512]{2,1,0:T(4,128)(2,1)} %param.20) | copy-start | bytes 24580
  14.9 4.2 %copy-start.13 = (s32[4]{0:T(128)S(1)}, s32[4]{0:T(128)}, u32[]{:S(2)}) copy-start(s32[4]{0:T(128)} %param.22) | copy-start | bytes 52
  14.9 4.3 %copy-start.3 = (bf16[4,4096]{1,0:T(4,128)(2,1)S(1)}, bf16[4,4096]{1,0:T(4,128)(2,1)}, u32[]{:S(2)}) copy-start(bf16[4,4096]{1,0:T(4,128)(2,1)} %param.19) | copy-start | bytes 98308
  70.4 19.9 %copy-start.14 = (s32[2]{0:T(128)S(1)}, s32[2]{0:T(128)}, u32[]{:S(2)}) copy-start(s32[2]{0:T(128)} %slice_reduce_fusion.1) | copy-start | bytes 28
  70.4 20.3 %copy-start.4 = (f32[4,2048]{1,0:T(4,128)S(1)}, f32[4,2048]{1,0:T(4,128)}, u32[]{:S(2)}) copy-start(f32[4,2048]{1,0:T(4,128)} %param.24) | copy-start | bytes 98308
  70.4 20.5 %copy-start.5 = (f32[2048]{0:T(1024)S(1)}, f32[2048]{0:T(1024)}, u32[]{:S(2)}) copy-start(f32[2048]{0:T(1024)} %param.25) | copy-start | bytes 24580
  70.4 29.8 %copy-start.11 = (pred[32,8]{0,1:T(8,128)(4,1)S(1)}, pred[32,8]{0,1:T(8,128)(4,1)}, u32[]{:S(2)}) copy-start(pred[32,8]{0,1:T(8,128)(4,1)} %get-tuple-element.219) | copy-start | bytes 772
  70.4 30.0 %copy-start.12 = (f32[32]{0:T(128)S(1)}, f32[32]{0:T(128)}, u32[]{:S(2)}) copy-start(f32[32]{0:T(128)} %compare_convert_fusion.2) | copy-start | bytes 388
  70.4 31.1 %copy-start.7 = (s32[32,8]{0,1:T(8,128)S(1)}, s32[32,8]{0,1:T(8,128)}, u32[]{:S(2)}) copy-start(s32[32,8]{0,1:T(8,128)} %param.27) | copy-start | bytes 3076
  105.7 2.9 copy-start.10
  107.4 262.2 %all-reduce.5.cloned.1.call-start = ((), (), s32[]{:S(2)}) async-start(), calls=%async_computation.1 | async-start | bytes 262144 | tf_op jit(solution)/shard_map/psum | solution.py:80
  230.8 3.0 copy-start.1
  230.8 3.0 copy-start.8
  230.8 12.4 %copy-start.2 = (bf16[1024,32]{0,1:T(8,128)(2,1)S(1)}, bf16[1024,32]{0,1:T(8,128)(2,1)}, u32[]{:S(2)}) copy-start(bf16[1024,32]{0,1:T(8,128)(2,1)} %param.32) | copy-start | bytes 196612
  230.9 12.7 %copy-start.9 = (s32[32,8]{0,1:T(8,128)S(1)}, s32[32,8]{0,1:T(8,128)}, u32[]{:S(2)}) copy-start(s32[32,8]{0,1:T(8,128)} %param.33) | copy-start | bytes 3076
Sparse Core Ops, SparseCore 0:
  107.5 122.4 all-reduce.2
  248.1 121.3 all-reduce.4
where the time goes:
time: 378 us
  waiting for transfers between devices  243 us (64%)
  blocking collectives  74.6 us (20%)
  matrix products  24.4 us (6%)
  local copies, waits for them, and re-layouts  15 us (4%)
  between operations  14.4 us (4%)
  other arithmetic  6.41 us (2%)
    psum x2, waiting for transfers between devices, expert_layer(): lax.psum(jnp.einsum('rec,ecw->rw', block, weighted, precision=lax.Precisi...  243 us
    all_gather x3, blocking collectives, joined(): everything = jax.tree.map(lambda part: lax.all_gather(part, axis), shard)  39.2 us
    all_gather x2, blocking collectives, expert_layer(): lax.all_gather(normed, 'exp', axis=0, tiled=True)  18.4 us
    psum x1, blocking collectives, on_device(): projected = lax.psum(head_term, 'seq')  17 us
    unnamed x34, local copies, waits for them, and re-layouts  8.47 us
  transfers between devices with their start and end apart: 2, of which 2 were waited for; matrix products, arithmetic and copies ran while one was open for 0% of the time, Pallas kernels for 0%

commit v1 on v0

v1 whole, which is shorter than its diff:
```python
import functools

import jax
import jax.numpy as jnp
from jax import lax
from jax.experimental import pallas as pl
from jax.experimental.pallas import tpu as pltpu
from jax.sharding import PartitionSpec as P

H = 32
KVH = 4
HD = 128
RB = 16
F32 = jnp.float32
BF16 = jnp.bfloat16
MESH = pl.DeviceIdType.MESH


def column_dot(x_ref, w_ref, start, width):
    return jnp.dot(x_ref[...], w_ref[:, pl.ds(start, width)], preferred_element_type=F32)


def normalise(x, gain):
    scale = lax.rsqrt(jnp.mean(x * x, axis=1, keepdims=True) + 1e-06)
    return (x * scale * gain).astype(BF16)


def own_gate(normed_ref, router_ref, ids_ref, me):
    logits = lax.dot_general(
        router_ref[...], normed_ref[...], (((1,), (1,)), ((), ())), preferred_element_type=F32
    )
    rows = logits.shape[1]
    labels = lax.broadcasted_iota(jnp.int32, logits.shape, 0)
    ids = ids_ref[...]
    hit = ids[0:1, :] == labels
    for k in range(1, ids.shape[0]):
        hit = jnp.logical_or(hit, ids[k : k + 1, :] == labels)
    sig = jnp.where(hit, jax.nn.sigmoid(logits), 0.0)
    total = jnp.sum(sig, axis=0, keepdims=True)
    own = jnp.sum(jnp.where(labels == me, sig, 0.0), axis=0, keepdims=True)
    gate = jnp.broadcast_to(own / total, (rows, rows))
    diag = lax.broadcasted_iota(jnp.int32, (rows, rows), 0) == lax.broadcasted_iota(
        jnp.int32, (rows, rows), 1
    )
    return jnp.sum(jnp.where(diag, gate, 0.0), axis=1, keepdims=True)


def kernel(
    nseq,
    nexp,
    q_hbm, nkv_hbm, kv_hbm, len_ref, wo_hbm, hid_hbm, g1_hbm, rt1_hbm, id1_hbm, gu1_hbm, dn1_hbm,
    tp_hbm, g2_hbm, rt2_hbm, id2_hbm, gu2_hbm, dn2_hbm,
    out1_ref, out2_ref,
    q, nkv, kbuf, vbuf, wo, hid, g1, rt1, id1, gu1, dn1, tp, g2, rt2, id2, gu2, dn2,
    q_stage, o_stage, l_stage, att_send, att_recv, att_stage,
    head_send, head_recv, state_tile, state_send, state_all, xn1, inner1, rep1, got1,
    thk_send, thk_all, thk_bf, talk_tiles, xn2, inner2, rep2, got2, fin_send, fin_recv,
    load_sem, kv_sem, send_sem, recv_sem,
):
    ndev = nseq * nexp
    s_me = lax.axis_index("seq")
    e_me = lax.axis_index("exp")
    me = s_me * nexp + e_me
    count = kbuf.shape[0]
    span = kbuf.shape[1]
    kw = kbuf.shape[2]
    d = wo.shape[1]
    dt = tp.shape[1]
    ff = dn1.shape[0]
    ft = dn2.shape[0]
    rows = nexp * count
    nrb = rows // RB
    eb = RB // count
    hp = H // nseq
    nct1, nct2 = d // 128, dt // 128
    nt1, nt2 = nrb * nct1, nrb * nct2
    stride1, stride2 = ndev // nt1, ndev // nt2

    loads = {}

    def load(name, src, dst):
        loads[name] = pltpu.make_async_copy(src, dst, load_sem.at[len(loads)])
        loads[name].start()

    load("q", q_hbm, q)
    load("nkv", nkv_hbm, nkv)
    kv_loads = []
    for c in range(count):
        pair = [
            pltpu.make_async_copy(kv_hbm.at[0, c], kbuf.at[c], kv_sem.at[2 * c]),
            pltpu.make_async_copy(kv_hbm.at[1, c], vbuf.at[c], kv_sem.at[2 * c + 1]),
        ]
        for copy in pair:
            copy.start()
        kv_loads.append(pair)
    load("wo", wo_hbm, wo)
    load("hid", hid_hbm, hid)
    load("g1", g1_hbm, g1)
    load("rt1", rt1_hbm, rt1)
    load("id1", id1_hbm, id1)
    load("gu1", gu1_hbm.at[0], gu1)
    load("dn1", dn1_hbm.at[0], dn1)
    load("tp", tp_hbm, tp)
    load("g2", g2_hbm, g2)
    load("rt2", rt2_hbm, rt2)
    load("id2", id2_hbm, id2)
    load("gu2", gu2_hbm.at[0], gu2)
    load("dn2", dn2_hbm.at[0], dn2)

    barrier = pltpu.get_barrier_semaphore()

    def greet(k, carry):
        dev = lax.rem(me + k, ndev)
        pl.semaphore_signal(barrier, inc=1, device_id=(dev // nexp, lax.rem(dev, nexp)), device_id_type=MESH)
        return carry

    lax.fori_loop(1, ndev, greet, 0)

    def remote(src, dst, phase, dev):
        return pltpu.make_async_remote_copy(
            src_ref=src,
            dst_ref=dst,
            send_sem=send_sem.at[phase],
            recv_sem=recv_sem.at[phase],
            device_id=(dev // nexp, lax.rem(dev, nexp)),
            device_id_type=MESH,
        )

    def send(src, dst, phase, dev):
        @pl.when(dev == me)
        def _():
            pltpu.make_async_copy(src, dst, recv_sem.at[phase]).start()

        @pl.when(dev != me)
        def _():
            remote(src, dst, phase, dev).start()

    def await_bytes(ref, sem):
        pltpu.make_async_copy(ref, ref, sem).wait()

    loads["q"].wait()
    loads["nkv"].wait()
    queries = q[...].astype(F32)
    for h in range(H):
        q_stage[h * 8 : h * 8 + count, :] = queries[:, h * HD : (h + 1) * HD]
    groups = H // KVH
    head_group = lax.broadcasted_iota(jnp.int32, (H, HD), 0) // groups
    places = s_me * span + lax.broadcasted_iota(jnp.int32, (1, span), 1)
    owner = s_me == 0
    scale = HD ** (-0.5)
    for c in range(count):
        q_c = q_stage[pl.ds(c, H, stride=8), :]
        spread = jnp.concatenate(
            [jnp.where(head_group == g, q_c, 0.0) for g in range(KVH)], axis=1
        )
        new_k = nkv[0, c : c + 1, :].astype(F32)
        new_v = nkv[1, c : c + 1, :].astype(F32)
        kv_loads[c][0].wait()
        scores = lax.dot_general(
            spread.astype(BF16), kbuf[c], (((1,), (1,)), ((), ())), preferred_element_type=F32
        ) * scale
        fresh = jnp.sum(spread * new_k, axis=1, keepdims=True) * scale
        fresh = jnp.where(owner, fresh, -1e30)
        valid = places < len_ref[c]
        masked = jnp.where(valid, scores, -1e30)
        peak = jnp.maximum(jnp.max(masked, axis=1, keepdims=True), fresh)
        weights = jnp.where(valid, jnp.exp(masked - peak), 0.0).astype(BF16)
        fresh_weight = jnp.where(owner, jnp.exp(fresh - peak), 0.0)
        total = jnp.sum(weights.astype(F32), axis=1, keepdims=True) + fresh_weight
        kv_loads[c][1].wait()
        mixed = jnp.dot(weights, vbuf[c], preferred_element_type=F32) + fresh_weight * new_v
        some = total > 0.0
        safe = jnp.where(some, total, 1.0)
        lse = jnp.where(some, peak + jnp.log(safe), -1e30)
        inverse = 1.0 / safe
        mixed = mixed * inverse
        lse = jnp.broadcast_to(lse, (H, HD))
        own = mixed[:, 0:HD]
        for g in range(1, KVH):
            own = jnp.where(head_group == g, mixed[:, g * HD : (g + 1) * HD], own)
        for t in range(nseq):
            o_stage[t, c * hp : (c + 1) * hp, :] = own[t * hp : (t + 1) * hp]
            l_stage[t, c * hp : (c + 1) * hp, :] = lse[t * hp : (t + 1) * hp]

    ar = count * hp
    diag = lax.broadcasted_iota(jnp.int32, (ar, HD), 0) == lax.broadcasted_iota(jnp.int32, (ar, HD), 1)
    part_row = lax.broadcasted_iota(jnp.int32, (RB, HD), 0)
    for t in range(nseq):
        att_send[t, 0:ar, :] = o_stage[t].astype(BF16)
        line = jnp.sum(jnp.where(diag, l_stage[t], 0.0), axis=0, keepdims=True)
        high = line.astype(BF16).astype(F32)
        mid = (line - high).astype(BF16).astype(F32)
        low = line - high - mid
        parts = jnp.where(part_row == 0, high, jnp.where(part_row == 1, mid, jnp.where(part_row == 2, low, 0.0)))
        att_send[t, ar : ar + RB, :] = parts.astype(BF16)
    pl.semaphore_wait(barrier, ndev - 1)
    for k in range(nseq):
        t = lax.rem(s_me + k, nseq)
        src, dst = att_send.at[t], att_recv.at[s_me]
        if k == 0:
            pltpu.make_async_copy(src, dst, recv_sem.at[0]).start()
        else:
            remote(src, dst, 0, t * nexp + e_me).start()
    await_bytes(att_recv, recv_sem.at[0])
    lses = []
    for t in range(nseq):
        parts = att_recv[t, ar : ar + RB, :].astype(F32)
        line = parts[0:1] + parts[1:2] + parts[2:3]
        lses.append(jnp.sum(jnp.where(diag, line, 0.0), axis=1, keepdims=True))
    top = functools.reduce(jnp.maximum, lses)
    shares = [jnp.exp(x - top) for x in lses]
    norm = 1.0 / functools.reduce(jnp.add, shares)
    attn = functools.reduce(
        jnp.add, [att_recv[t, 0:ar, :].astype(F32) * (shares[t] * norm) for t in range(nseq)]
    )
    att_stage[...] = attn
    heads = jnp.concatenate(
        [att_stage[pl.ds(j, count, stride=hp), :] for j in range(hp)], axis=1
    ).astype(BF16)

    loads["wo"].wait()
    loads["hid"].wait()
    wide = 512
    for i in range(d // wide):
        at = i * wide
        term = jnp.dot(heads, wo[:, at : at + wide], preferred_element_type=F32)
        term = term + jnp.where(owner, hid[:, at : at + wide], 0.0)
        for j in range(wide // 128):
            head_send[at // 128 + j] = term[:, j * 128 : (j + 1) * 128]
    my_block = e_me // eb

    def send_terms(k, carry):
        ct = lax.rem(e_me * 2 + s_me + k, nct1)
        dev = (my_block * nct1 + ct) * stride1
        send(head_send.at[ct], head_recv.at[s_me * eb + lax.rem(e_me, eb)], 1, dev)
        return carry

    lax.fori_loop(0, nct1, send_terms, 0)
    tile1 = me // stride1
    owns1 = jnp.logical_and(lax.rem(me, stride1) == 0, tile1 < nt1)

    def send_state(k, carry):
        dev = lax.rem(me + k, ndev)
        remote(state_send, state_all.at[tile1], 2, dev).start()
        return carry

    @pl.when(owns1)
    def _():
        await_bytes(head_recv, recv_sem.at[1])
        for b in range(eb):
            state_tile[b * count : (b + 1) * count, :] = functools.reduce(
                jnp.add, [head_recv[t * eb + b] for t in range(nseq)]
            )
        state_send[...] = state_tile[...].astype(BF16)
        pltpu.make_async_copy(state_send, state_all.at[tile1], recv_sem.at[2]).start()
        lax.fori_loop(1, ndev, send_state, 0)

    def assemble(tiles, nct):
        return jnp.concatenate(
            [
                jnp.concatenate([tiles[b * nct + c].astype(F32) for c in range(nct)], axis=1)
                for b in range(nrb)
            ],
            axis=0,
        )

    def experts(xn, router, ids, gu, dn, inner, rep, width, hidden, nct):
        gate = own_gate(xn, router, ids, me)
        step = 256 if hidden % 256 == 0 else 128
        for i in range(hidden // step):
            a = column_dot(xn, gu, i * step, step)
            b = column_dot(xn, gu, hidden + i * step, step)
            inner[:, i * step : (i + 1) * step] = (a * jax.nn.sigmoid(a) * b).astype(BF16)
        for i in range(width // 256):
            y = column_dot(inner, dn, i * 256, 256).astype(BF16).astype(F32)
            y = jnp.where(gate > 0.0, gate * y, 0.0).astype(BF16)
            for r in range(nrb):
                for j in range(2):
                    rep[r * nct + i * 2 + j] = y[r * RB : (r + 1) * RB, j * 128 : (j + 1) * 128]

    def scatter(rep, got, nt, stride, phase):
        def one(k, carry):
            t = lax.rem(me // stride + k, nt)
            send(rep.at[t], got.at[me], phase, t * stride)
            return carry

        lax.fori_loop(0, nt, one, 0)

    def gather_sum(got):
        return functools.reduce(jnp.add, [got[i].astype(F32) for i in range(ndev)])

    loads["g1"].wait()
    loads["rt1"].wait()
    loads["id1"].wait()
    await_bytes(state_all, recv_sem.at[2])
    xn1[...] = normalise(assemble(state_all, nct1), g1[...])
    loads["gu1"].wait()
    loads["dn1"].wait()
    experts(xn1, rt1, id1, gu1, dn1, inner1, rep1, d, ff, nct1)
    scatter(rep1, got1, nt1, stride1, 3)

    def send_thinker(k, carry):
        dev = lax.rem(me + k, ndev)
        remote(thk_send, thk_all.at[tile1], 4, dev).start()
        return carry

    @pl.when(owns1)
    def _():
        await_bytes(got1, recv_sem.at[3])
        thk_send[...] = (state_tile[...] + gather_sum(got1)).astype(BF16)
        pltpu.make_async_copy(thk_send, thk_all.at[tile1], recv_sem.at[4]).start()
        lax.fori_loop(1, ndev, send_thinker, 0)

    loads["tp"].wait()
    loads["g2"].wait()
    loads["rt2"].wait()
    loads["id2"].wait()
    await_bytes(thk_all, recv_sem.at[4])
    thinker = assemble(thk_all, nct1)
    thk_bf[...] = thinker.astype(BF16)
    talk_parts = []
    for i in range(dt // 256):
        y = column_dot(thk_bf, tp, i * 256, 256)
        talk_parts.append(y)
        for r in range(nrb):
            for j in range(2):
                talk_tiles[r * nct2 + i * 2 + j] = y[r * RB : (r + 1) * RB, j * 128 : (j + 1) * 128]
    xn2[...] = normalise(jnp.concatenate(talk_parts, axis=1), g2[...])
    loads["gu2"].wait()
    loads["dn2"].wait()
    experts(xn2, rt2, id2, gu2, dn2, inner2, rep2, dt, ft, nct2)
    scatter(rep2, got2, nt2, stride2, 5)

    block = e_me // eb
    place = lax.rem(e_me, eb)
    mine = jnp.zeros((count, d), F32)
    for b in range(nrb):
        for k in range(eb):
            at = b * RB + k * count
            here = jnp.logical_and(block == b, place == k)
            mine = jnp.where(here, thinker[at : at + count], mine)
    out1_ref[...] = mine

    tile2 = me // stride2
    owns2 = jnp.logical_and(lax.rem(me, stride2) == 0, tile2 < nt2)
    block2, column2 = tile2 // nct2, lax.rem(tile2, nct2)

    def send_final(k, carry):
        to = lax.rem(me + k, nseq * eb)
        seq_to, at = to // eb, lax.rem(to, eb)
        send(fin_send.at[at], fin_recv.at[column2], 6, seq_to * nexp + block2 * eb + at)
        return carry

    @pl.when(owns2)
    def _():
        await_bytes(got2, recv_sem.at[5])
        tile = talk_tiles[tile2] + gather_sum(got2)
        for b in range(eb):
            fin_send[b] = tile[b * count : (b + 1) * count]
        lax.fori_loop(0, nseq * eb, send_final, 0)

    await_bytes(att_send.at[pl.ds(0, nseq - 1)], send_sem.at[0])
    for phase, sent, total, inside in (
        (1, head_send, nct1, jnp.logical_and(owns1, tile1 // nct1 == my_block)),
        (3, rep1, nt1, owns1),
        (5, rep2, nt2, owns2),
    ):

        @pl.when(inside)
        def _():
            await_bytes(sent.at[pl.ds(0, total - 1)], send_sem.at[phase])

        @pl.when(jnp.logical_not(inside))
        def _():
            await_bytes(sent.at[pl.ds(0, total)], send_sem.at[phase])

    @pl.when(owns1)
    def _():
        await_bytes(got1.at[pl.ds(0, ndev - 1)], send_sem.at[2])
        await_bytes(got1.at[pl.ds(0, ndev - 1)], send_sem.at[4])

    @pl.when(owns2)
    def _():
        @pl.when(e_me // eb == block2)
        def _():
            await_bytes(head_recv.at[pl.ds(0, nseq * eb - 1)], send_sem.at[6])

        @pl.when(e_me // eb != block2)
        def _():
            await_bytes(head_recv, send_sem.at[6])

    await_bytes(fin_recv, recv_sem.at[6])
    for j in range(nct2):
        out2_ref[:, j * 128 : (j + 1) * 128] = fin_recv[j]


def on_device(
    queries, new_kv, kv_cache, lengths, out_proj, hidden_in, norm_gain, router, expert_ids,
    w_gate_up, w_down, talk_proj, talk_gain, talk_router, talk_ids, talk_gate_up, talk_down,
):
    nseq, nexp = lax.axis_size("seq"), lax.axis_size("exp")
    ndev = nseq * nexp
    count = queries.shape[0]
    span, kw = kv_cache.shape[2:]
    d, dt = talk_proj.shape
    ff, ft = w_down.shape[1], talk_down.shape[1]
    rows = nexp * count
    nrb = rows // RB
    eb = RB // count
    hp = H // nseq
    nct1, nct2 = d // 128, dt // 128
    nt1, nt2 = nrb * nct1, nrb * nct2
    ar = count * hp
    any_spec = pl.BlockSpec(memory_space=pl.ANY)
    vmem_spec = pl.BlockSpec(memory_space=pltpu.VMEM)
    args = (
        queries, new_kv, kv_cache, lengths, out_proj, hidden_in, norm_gain.reshape(1, d), router.T,
        expert_ids.T, w_gate_up, w_down, talk_proj, talk_gain.reshape(1, dt), talk_router.T,
        talk_ids.T, talk_gate_up, talk_down,
    )
    in_specs = [any_spec] * len(args)
    in_specs[3] = pl.BlockSpec(memory_space=pltpu.SMEM)
    own = lambda x, drop=0: pltpu.VMEM(x.shape[drop:], x.dtype)
    scratch = [
        own(args[0]), own(args[1]),
        pltpu.VMEM((count, span, kw), BF16), pltpu.VMEM((count, span, kw), BF16),
        own(args[4]), own(args[5]), own(args[6]), own(args[7]), own(args[8]),
        own(args[9], 1), own(args[10], 1), own(args[11]), own(args[12]), own(args[13]), own(args[14]),
        own(args[15], 1), own(args[16], 1),
        pltpu.VMEM((H * 8, HD), F32),
        pltpu.VMEM((nseq, ar, HD), F32), pltpu.VMEM((nseq, ar, HD), F32),
        pltpu.VMEM((nseq, ar + RB, HD), BF16), pltpu.VMEM((nseq, ar + RB, HD), BF16),
        pltpu.VMEM((ar, HD), F32),
        pltpu.VMEM((nct1, count, 128), F32), pltpu.VMEM((nseq * eb, count, 128), F32),
        pltpu.VMEM((RB, 128), F32), pltpu.VMEM((RB, 128), BF16),
        pltpu.VMEM((nt1, RB, 128), BF16),
        pltpu.VMEM((rows, d), BF16), pltpu.VMEM((rows, ff), BF16),
        pltpu.VMEM((nt1, RB, 128), BF16), pltpu.VMEM((ndev, RB, 128), BF16),
        pltpu.VMEM((RB, 128), BF16), pltpu.VMEM((nt1, RB, 128), BF16),
        pltpu.VMEM((rows, d), BF16),
        pltpu.VMEM((nt2, RB, 128), F32),
        pltpu.VMEM((rows, dt), BF16), pltpu.VMEM((rows, ft), BF16),
        pltpu.VMEM((nt2, RB, 128), BF16), pltpu.VMEM((ndev, RB, 128), BF16),
        pltpu.VMEM((eb, count, 128), F32), pltpu.VMEM((nct2, count, 128), F32),
        pltpu.SemaphoreType.DMA((16,)),
        pltpu.SemaphoreType.DMA((2 * count,)),
        pltpu.SemaphoreType.DMA((7,)),
        pltpu.SemaphoreType.DMA((7,)),
    ]
    return pl.pallas_call(
        functools.partial(kernel, nseq, nexp),
        out_shape=(
            jax.ShapeDtypeStruct((count, d), F32),
            jax.ShapeDtypeStruct((count, dt), F32),
        ),
        in_specs=in_specs,
        out_specs=(vmem_spec, vmem_spec),
        scratch_shapes=scratch,
        compiler_params=pltpu.CompilerParams(
            collective_id=0, has_side_effects=True, vmem_limit_bytes=56 * 1024 * 1024
        ),
    )(*args)


def solution(mesh):
    placed = (
        P("exp", None),
        P(None, "exp", None),
        P(None, "exp", "seq", None),
        P("exp"),
        P("seq", None),
        P("exp", None),
        P(),
        P(),
        P(),
        P(("seq", "exp"), None, None),
        P(("seq", "exp"), None, None),
        P(),
        P(),
        P(),
        P(),
        P(("seq", "exp"), None, None),
        P(("seq", "exp"), None, None),
    )
    return jax.shard_map(
        on_device,
        mesh=mesh,
        in_specs=placed,
        out_specs=(P("exp", None), P("exp", None)),
        check_vma=False,
    )
```

time: 378 us -> 53.9 us (0.14)
  waiting for transfers between devices: 243 us -> 0 us
  blocking collectives: 74.6 us -> 0 us
  Pallas kernels: 0 us -> 50.3 us
  matrix products: 24.4 us -> 0 us
  between operations: 14.4 us -> 0.65 us
  local copies, waits for them, and re-layouts: 15 us -> 2.7 us
  other arithmetic: 6.41 us -> 0 us
    psum x2 -> x0, waiting for transfers between devices: 243 us -> none  [expert_layer(): lax.psum(jnp.einsum('rec,ecw->rw', block, weighted, precision=lax.Precisi...]
    all_gather x5 -> x0, blocking collectives: 57.6 us -> none  [the longest x3 39.2 us: joined(): everything = jax.tree.map(lambda part: lax.all_gather(part, axis), shard)]
    pallas_call x0 -> x1, Pallas kernels: none -> 50.3 us  [on_device(): pl.pallas_call(functools.partial(kernel, nseq, nexp), out_shape=(jax.Shap...]
    dot_general x18 -> x0, matrix products: 24.4 us -> none  [the longest x2 5.44 us: expert_layer(): jnp.einsum('ecw,ewf->ecf', slot_rows, gate_up, preferred_element_type=jnp...]
    psum x1 -> x0, blocking collectives: 17 us -> none  [on_device(): projected = lax.psum(head_term, 'seq')]
    unnamed x34 -> x2, local copies, waits for them, and re-layouts: 8.47 us -> 2.7 us
    slice x2 -> x0, local copies, waits for them, and re-layouts: 5.13 us -> none  [the longest x1 4.42 us: local_attention(): values = kv_cache[1].reshape(count, span, KVH, HD)]
  transfers between devices with their start and end apart: 2 -> 0, of which waited for: 2 -> 0; matrix products, arithmetic and copies ran while one was open for 0% -> 0% of each run, Pallas kernels for 0% -> 0%
where the time goes in v1:
time: 53.9 us; the launch traced here: 53.7 us
  Pallas kernels  50.3 us (93%)
  local copies, waits for them, and re-layouts  2.7 us (5%)
  between operations  0.65 us (1%)
    pallas_call x1, Pallas kernels, on_device(): pl.pallas_call(functools.partial(kernel, nseq, nexp), out_shape=(jax.Shap...  50.3 us
    unnamed x2, local copies, waits for them, and re-layouts  2.7 us

profile of v1, /device:TPU:0, one launch (start us, length us, event | category | flops | bytes accessed | tf_op | source)
XLA Modules:
  0.0 53.7 jit_solution(9628907609766557822)
XLA Ops:
  0.6 50.3 %shard_map.176 = (f32[4,2048]{1,0:T(4,128)}, f32[4,1024]{1,0:T(4,128)}) custom-call(bf16[4,4096]{1,0:T(4,128)(2,1)} %q_hbm.1, bf16[2,4,512]{2,1,0:T(4,128)(2,1)} %nkv_hbm.1, bf16[2,4,512,512]{3,2,1,0:T(8,128)(2,1)} %kv_hbm.1, s32[4]{0:T(128)} %len_ref.1, bf16[1024,2048]{1,0:T(8,128)(2,1)} %wo_hbm.1, f32[4,2048]{1,0:T(4,128)} %hid_hbm.1, f32[1,2048]{1,0:T(1,128)} %bitcast.8, ...), custom_call_target="tpu_custom_call" | custom-call | tf_op jit(solution)/shard_map/pallas_call | solution.py:450
  51.0 1.4 %copy.21 = f32[4,2048]{1,0:T(4,128)} copy(f32[4,2048]{1,0:T(4,128)} %get-tuple-element.4) | data formatting | bytes 65536
  52.4 1.3 %copy.22 = f32[4,1024]{1,0:T(4,128)} copy(f32[4,1024]{1,0:T(4,128)} %get-tuple-element.5) | data formatting | bytes 32768

commit v2 on v1

v2 whole, which is shorter than its diff:
```python
import functools

import jax
import jax.numpy as jnp
from jax import lax
from jax.experimental import pallas as pl
from jax.experimental.pallas import tpu as pltpu
from jax.sharding import PartitionSpec as P

H = 32
KVH = 4
HD = 128
RB = 16
F32 = jnp.float32
BF16 = jnp.bfloat16
MESH = pl.DeviceIdType.MESH


def column_dot(x_ref, w_ref, start, width):
    return jnp.dot(x_ref[...], w_ref[:, pl.ds(start, width)], preferred_element_type=F32)


def normalise(x, gain):
    scale = lax.rsqrt(jnp.mean(x * x, axis=1, keepdims=True) + 1e-06)
    return (x * scale * gain).astype(BF16)


def own_gate(normed_ref, router_ref, ids_ref, me):
    logits = lax.dot_general(
        router_ref[...], normed_ref[...], (((1,), (1,)), ((), ())), preferred_element_type=F32
    )
    rows = logits.shape[1]
    labels = lax.broadcasted_iota(jnp.int32, logits.shape, 0)
    ids = ids_ref[...]
    hit = ids[0:1, :] == labels
    for k in range(1, ids.shape[0]):
        hit = jnp.logical_or(hit, ids[k : k + 1, :] == labels)
    sig = jnp.where(hit, jax.nn.sigmoid(logits), 0.0)
    total = jnp.sum(sig, axis=0, keepdims=True)
    own = jnp.sum(jnp.where(labels == me, sig, 0.0), axis=0, keepdims=True)
    gate = jnp.broadcast_to(own / total, (rows, rows))
    diag = lax.broadcasted_iota(jnp.int32, (rows, rows), 0) == lax.broadcasted_iota(
        jnp.int32, (rows, rows), 1
    )
    return jnp.sum(jnp.where(diag, gate, 0.0), axis=1, keepdims=True)


def kernel(
    nseq,
    nexp,
    q_hbm, nkv_hbm, kv_hbm, len_ref, wo_hbm, hid_hbm, g1_hbm, rt1_hbm, id1_hbm, gu1_hbm, dn1_hbm,
    tp_hbm, g2_hbm, rt2_hbm, id2_hbm, gu2_hbm, dn2_hbm,
    out1_ref, out2_ref,
    q, nkv, kbuf, vbuf, wo, hid, g1, rt1, id1, gu1, dn1, tp, g2, rt2, id2, gu2, dn2,
    q_stage, o_stage, l_stage, att_send, att_recv, att_stage,
    terms, state_all, xn1, inner1, rep1, got1, part1, talk_all, xn2, inner2, rep2, got2, part2,
    load_sem, kv_sem, send_sem, recv_sem,
):
    s_me = lax.axis_index("seq")
    e_me = lax.axis_index("exp")
    me = s_me * nexp + e_me
    count = kbuf.shape[0]
    span = kbuf.shape[1]
    kw = kbuf.shape[2]
    d = wo.shape[1]
    dt = tp.shape[1]
    ff = dn1.shape[0]
    ft = dn2.shape[0]
    hp = H // nseq
    stack = RB // count

    loads = {}

    def load(name, src, dst):
        loads[name] = pltpu.make_async_copy(src, dst, load_sem.at[len(loads)])
        loads[name].start()

    load("q", q_hbm, q)
    load("nkv", nkv_hbm, nkv)
    kv_loads = []
    for c in range(count):
        pair = [
            pltpu.make_async_copy(kv_hbm.at[0, c], kbuf.at[c], kv_sem.at[2 * c]),
            pltpu.make_async_copy(kv_hbm.at[1, c], vbuf.at[c], kv_sem.at[2 * c + 1]),
        ]
        for copy in pair:
            copy.start()
        kv_loads.append(pair)
    load("wo", wo_hbm, wo)
    load("hid", hid_hbm, hid)
    load("g1", g1_hbm, g1)
    load("rt1", rt1_hbm, rt1)
    load("id1", id1_hbm, id1)
    load("gu1", gu1_hbm.at[0], gu1)
    load("dn1", dn1_hbm.at[0], dn1)
    load("tp", tp_hbm, tp)
    load("g2", g2_hbm, g2)
    load("rt2", rt2_hbm, rt2)
    load("id2", id2_hbm, id2)
    load("gu2", gu2_hbm.at[0], gu2)
    load("dn2", dn2_hbm.at[0], dn2)

    barrier = pltpu.get_barrier_semaphore()

    def along_seq(k):
        return (lax.rem(s_me + k, nseq), e_me)

    def along_exp(k):
        return (s_me, lax.rem(e_me + k, nexp))

    partners = [along_seq(k) for k in range(1, nseq)] + [along_exp(k) for k in range(1, nexp)]
    for dev in partners:
        pl.semaphore_signal(barrier, inc=1, device_id=dev, device_id_type=MESH)

    def remote(src, dst, phase, dev):
        return pltpu.make_async_remote_copy(
            src_ref=src,
            dst_ref=dst,
            send_sem=send_sem.at[phase],
            recv_sem=recv_sem.at[phase],
            device_id=dev,
            device_id_type=MESH,
        )

    def await_bytes(ref, sem):
        pltpu.make_async_copy(ref, ref, sem).wait()

    def gather(buf, phase, me_at, along, ways):
        for k in range(1, ways):
            remote(buf.at[me_at], buf.at[me_at], phase, along(k)).start()
        await_bytes(buf.at[pl.ds(0, ways - 1)], recv_sem.at[phase])

    def scatter(src, dst, phase, me_at, along, ways, axis):
        for k in range(1, ways):
            dev = along(k)
            remote(src.at[dev[axis]], dst.at[me_at], phase, dev).start()
        dst[me_at] = src[me_at]
        await_bytes(dst.at[pl.ds(0, ways - 1)], recv_sem.at[phase])

    def pack(x):
        return [
            jnp.concatenate(
                [x[:, (i * stack + k) * 128 : (i * stack + k + 1) * 128] for k in range(stack)], axis=0
            ).astype(BF16)
            for i in range(x.shape[1] // (128 * stack))
        ]

    def unpack(tiles):
        return jnp.concatenate(
            [t[k * count : (k + 1) * count] for t in tiles for k in range(stack)], axis=1
        )

    def summed(buf, ways):
        return [
            functools.reduce(jnp.add, [buf[w, i].astype(F32) for w in range(ways)])
            for i in range(buf.shape[1])
        ]

    def all_rows(buf, out):
        for i in range(buf.shape[1]):
            tiles = [buf[e, i].astype(F32) for e in range(nexp)]
            for k in range(stack):
                at = (i * stack + k) * 128
                out[:, at : at + 128] = jnp.concatenate(
                    [t[k * count : (k + 1) * count] for t in tiles], axis=0
                ).astype(BF16)

    loads["q"].wait()
    loads["nkv"].wait()
    queries = q[...].astype(F32)
    for h in range(H):
        q_stage[h * 8 : h * 8 + count, :] = queries[:, h * HD : (h + 1) * HD]
    groups = H // KVH
    head_group = lax.broadcasted_iota(jnp.int32, (H, HD), 0) // groups
    places = s_me * span + lax.broadcasted_iota(jnp.int32, (1, span), 1)
    owner = s_me == 0
    scale = HD ** (-0.5)
    for c in range(count):
        q_c = q_stage[pl.ds(c, H, stride=8), :]
        spread = jnp.concatenate(
            [jnp.where(head_group == g, q_c, 0.0) for g in range(KVH)], axis=1
        )
        new_k = nkv[0, c : c + 1, :].astype(F32)
        new_v = nkv[1, c : c + 1, :].astype(F32)
        kv_loads[c][0].wait()
        scores = lax.dot_general(
            spread.astype(BF16), kbuf[c], (((1,), (1,)), ((), ())), preferred_element_type=F32
        ) * scale
        fresh = jnp.sum(spread * new_k, axis=1, keepdims=True) * scale
        fresh = jnp.where(owner, fresh, -1e30)
        valid = places < len_ref[c]
        masked = jnp.where(valid, scores, -1e30)
        peak = jnp.maximum(jnp.max(masked, axis=1, keepdims=True), fresh)
        weights = jnp.where(valid, jnp.exp(masked - peak), 0.0).astype(BF16)
        fresh_weight = jnp.where(owner, jnp.exp(fresh - peak), 0.0)
        total = jnp.sum(weights.astype(F32), axis=1, keepdims=True) + fresh_weight
        kv_loads[c][1].wait()
        mixed = jnp.dot(weights, vbuf[c], preferred_element_type=F32) + fresh_weight * new_v
        some = total > 0.0
        safe = jnp.where(some, total, 1.0)
        lse = jnp.where(some, peak + jnp.log(safe), -1e30)
        inverse = 1.0 / safe
        mixed = mixed * inverse
        lse = jnp.broadcast_to(lse, (H, HD))
        own = mixed[:, 0:HD]
        for g in range(1, KVH):
            own = jnp.where(head_group == g, mixed[:, g * HD : (g + 1) * HD], own)
        for t in range(nseq):
            o_stage[t, c * hp : (c + 1) * hp, :] = own[t * hp : (t + 1) * hp]
            l_stage[t, c * hp : (c + 1) * hp, :] = lse[t * hp : (t + 1) * hp]

    ar = count * hp
    diag = lax.broadcasted_iota(jnp.int32, (ar, HD), 0) == lax.broadcasted_iota(jnp.int32, (ar, HD), 1)
    part_row = lax.broadcasted_iota(jnp.int32, (RB, HD), 0)
    for t in range(nseq):
        att_send[t, 0:ar, :] = o_stage[t].astype(BF16)
        line = jnp.sum(jnp.where(diag, l_stage[t], 0.0), axis=0, keepdims=True)
        high = line.astype(BF16).astype(F32)
        mid = (line - high).astype(BF16).astype(F32)
        low = line - high - mid
        parts = jnp.where(part_row == 0, high, jnp.where(part_row == 1, mid, jnp.where(part_row == 2, low, 0.0)))
        att_send[t, ar : ar + RB, :] = parts.astype(BF16)
    pl.semaphore_wait(barrier, nseq + nexp - 2)
    scatter(att_send, att_recv, 0, s_me, along_seq, nseq, 0)
    lses = []
    for t in range(nseq):
        parts = att_recv[t, ar : ar + RB, :].astype(F32)
        line = parts[0:1] + parts[1:2] + parts[2:3]
        lses.append(jnp.sum(jnp.where(diag, line, 0.0), axis=1, keepdims=True))
    top = functools.reduce(jnp.maximum, lses)
    shares = [jnp.exp(x - top) for x in lses]
    norm = 1.0 / functools.reduce(jnp.add, shares)
    attn = functools.reduce(
        jnp.add, [att_recv[t, 0:ar, :].astype(F32) * (shares[t] * norm) for t in range(nseq)]
    )
    att_stage[...] = attn
    heads = jnp.concatenate(
        [att_stage[pl.ds(j, count, stride=hp), :] for j in range(hp)], axis=1
    ).astype(BF16)

    loads["wo"].wait()
    wide = 128 * stack
    for i in range(d // wide):
        term = jnp.dot(heads, wo[:, i * wide : (i + 1) * wide], preferred_element_type=F32)
        terms[s_me, i] = pack(term)[0]
    gather(terms, 1, s_me, along_seq, nseq)
    loads["hid"].wait()
    loads["g1"].wait()
    state = hid[...] + unpack(summed(terms, nseq))

    def experts(xn, router, ids, gu, dn, inner, rep, width, hidden):
        gate = own_gate(xn, router, ids, me)
        step = 256 if hidden % 256 == 0 else 128
        for i in range(hidden // step):
            a = column_dot(xn, gu, i * step, step)
            b = column_dot(xn, gu, hidden + i * step, step)
            inner[:, i * step : (i + 1) * step] = (a * jax.nn.sigmoid(a) * b).astype(BF16)
        for i in range(width // wide):
            y = column_dot(inner, dn, i * wide, wide).astype(BF16).astype(F32)
            y = jnp.where(gate > 0.0, gate * y, 0.0)
            for e in range(nexp):
                rep[e, i] = pack(y[e * count : (e + 1) * count])[0]

    def layer(stream, gain, everyone, xn, router, ids, gu, dn, inner, rep, got, part, phase, names):
        for i, tile in enumerate(pack(normalise(stream, gain).astype(F32))):
            everyone[e_me, i] = tile
        gather(everyone, phase, e_me, along_exp, nexp)
        all_rows(everyone, xn)
        for name in names:
            loads[name].wait()
        experts(xn, router, ids, gu, dn, inner, rep, stream.shape[1], inner.shape[1])
        scatter(rep, got, phase + 1, e_me, along_exp, nexp, 1)
        for i, tile in enumerate(summed(got, nexp)):
            part[s_me, i] = tile.astype(BF16)
        gather(part, phase + 2, s_me, along_seq, nseq)
        return stream + unpack(summed(part, nseq))

    thinker = layer(
        state, g1[...], state_all, xn1, rt1, id1, gu1, dn1, inner1, rep1, got1, part1, 2,
        ("rt1", "id1", "gu1", "dn1"),
    )
    out1_ref[...] = thinker
    loads["tp"].wait()
    loads["g2"].wait()
    thinker_bf = thinker.astype(BF16)
    talk_in = jnp.concatenate(
        [
            jnp.dot(thinker_bf, tp[:, i * wide : (i + 1) * wide], preferred_element_type=F32)
            for i in range(dt // wide)
        ],
        axis=1,
    )
    out2_ref[...] = layer(
        talk_in, g2[...], talk_all, xn2, rt2, id2, gu2, dn2, inner2, rep2, got2, part2, 5,
        ("rt2", "id2", "gu2", "dn2"),
    )

    for phase, buf, ways in (
        (0, att_send, nseq),
        (1, terms, nseq),
        (2, state_all, nexp),
        (3, rep1, nexp),
        (4, part1, nseq),
        (5, talk_all, nexp),
        (6, rep2, nexp),
        (7, part2, nseq),
    ):
        await_bytes(buf.at[pl.ds(0, ways - 1)], send_sem.at[phase])


def on_device(
    queries, new_kv, kv_cache, lengths, out_proj, hidden_in, norm_gain, router, expert_ids,
    w_gate_up, w_down, talk_proj, talk_gain, talk_router, talk_ids, talk_gate_up, talk_down,
):
    nseq, nexp = lax.axis_size("seq"), lax.axis_size("exp")
    count = queries.shape[0]
    span, kw = kv_cache.shape[2:]
    d, dt = talk_proj.shape
    ff, ft = w_down.shape[1], talk_down.shape[1]
    rows = nexp * count
    hp = H // nseq
    ar = count * hp
    wide = 128 * (RB // count)
    any_spec = pl.BlockSpec(memory_space=pl.ANY)
    vmem_spec = pl.BlockSpec(memory_space=pltpu.VMEM)
    args = (
        queries, new_kv, kv_cache, lengths, out_proj, hidden_in, norm_gain.reshape(1, d), router.T,
        expert_ids.T, w_gate_up, w_down, talk_proj, talk_gain.reshape(1, dt), talk_router.T,
        talk_ids.T, talk_gate_up, talk_down,
    )
    in_specs = [any_spec] * len(args)
    in_specs[3] = pl.BlockSpec(memory_space=pltpu.SMEM)
    own = lambda x, drop=0: pltpu.VMEM(x.shape[drop:], x.dtype)
    scratch = [
        own(args[0]), own(args[1]),
        pltpu.VMEM((count, span, kw), BF16), pltpu.VMEM((count, span, kw), BF16),
        own(args[4]), own(args[5]), own(args[6]), own(args[7]), own(args[8]),
        own(args[9], 1), own(args[10], 1), own(args[11]), own(args[12]), own(args[13]), own(args[14]),
        own(args[15], 1), own(args[16], 1),
        pltpu.VMEM((H * 8, HD), F32),
        pltpu.VMEM((nseq, ar, HD), F32), pltpu.VMEM((nseq, ar, HD), F32),
        pltpu.VMEM((nseq, ar + RB, HD), BF16), pltpu.VMEM((nseq, ar + RB, HD), BF16),
        pltpu.VMEM((ar, HD), F32),
        pltpu.VMEM((nseq, d // wide, RB, 128), BF16),
        pltpu.VMEM((nexp, d // wide, RB, 128), BF16),
        pltpu.VMEM((rows, d), BF16), pltpu.VMEM((rows, ff), BF16),
        pltpu.VMEM((nexp, d // wide, RB, 128), BF16), pltpu.VMEM((nexp, d // wide, RB, 128), BF16),
        pltpu.VMEM((nseq, d // wide, RB, 128), BF16),
        pltpu.VMEM((nexp, dt // wide, RB, 128), BF16),
        pltpu.VMEM((rows, dt), BF16), pltpu.VMEM((rows, ft), BF16),
        pltpu.VMEM((nexp, dt // wide, RB, 128), BF16), pltpu.VMEM((nexp, dt // wide, RB, 128), BF16),
        pltpu.VMEM((nseq, dt // wide, RB, 128), BF16),
        pltpu.SemaphoreType.DMA((16,)),
        pltpu.SemaphoreType.DMA((2 * count,)),
        pltpu.SemaphoreType.DMA((8,)),
        pltpu.SemaphoreType.DMA((8,)),
    ]
    return pl.pallas_call(
        functools.partial(kernel, nseq, nexp),
        out_shape=(
            jax.ShapeDtypeStruct((count, d), F32),
            jax.ShapeDtypeStruct((count, dt), F32),
        ),
        in_specs=in_specs,
        out_specs=(vmem_spec, vmem_spec),
        scratch_shapes=scratch,
        compiler_params=pltpu.CompilerParams(
            collective_id=0, has_side_effects=True, vmem_limit_bytes=56 * 1024 * 1024
        ),
    )(*args)


def solution(mesh):
    placed = (
        P("exp", None),
        P(None, "exp", None),
        P(None, "exp", "seq", None),
        P("exp"),
        P("seq", None),
        P("exp", None),
        P(),
        P(),
        P(),
        P(("seq", "exp"), None, None),
        P(("seq", "exp"), None, None),
        P(),
        P(),
        P(),
        P(),
        P(("seq", "exp"), None, None),
        P(("seq", "exp"), None, None),
    )
    return jax.shard_map(
        on_device,
        mesh=mesh,
        in_specs=placed,
        out_specs=(P("exp", None), P("exp", None)),
        check_vma=False,
    )
```

time: 53.9 us -> 48.3 us (0.90)
  Pallas kernels: 50.3 us -> 44.7 us
    pallas_call x1, Pallas kernels: 50.3 us -> 44.7 us  [on_device(): pl.pallas_call(functools.partial(kernel, nseq, nexp), out_shape=(jax.Shap...]
where the time goes in v2:
time: 48.3 us; the launch traced here: 48.1 us
  Pallas kernels  44.7 us (93%)
  local copies, waits for them, and re-layouts  2.7 us (6%)
  between operations  0.65 us (1%)
    pallas_call x1, Pallas kernels, on_device(): pl.pallas_call(functools.partial(kernel, nseq, nexp), out_shape=(jax.Shap...  44.7 us
    unnamed x2, local copies, waits for them, and re-layouts  2.7 us

profile of v2, /device:TPU:0, one launch (start us, length us, event | category | flops | bytes accessed | tf_op | source)
XLA Modules:
  0.0 48.1 jit_solution(8220641663524488976)
XLA Ops:
  0.6 44.7 %shard_map.176 = (f32[4,2048]{1,0:T(4,128)}, f32[4,1024]{1,0:T(4,128)}) custom-call(bf16[4,4096]{1,0:T(4,128)(2,1)} %q_hbm.1, bf16[2,4,512]{2,1,0:T(4,128)(2,1)} %nkv_hbm.1, bf16[2,4,512,512]{3,2,1,0:T(8,128)(2,1)} %kv_hbm.1, s32[4]{0:T(128)} %len_ref.1, bf16[1024,2048]{1,0:T(8,128)(2,1)} %wo_hbm.1, f32[4,2048]{1,0:T(4,128)} %hid_hbm.1, f32[1,2048]{1,0:T(1,128)} %bitcast.8, ...), custom_call_target="tpu_custom_call" | custom-call | tf_op jit(solution)/shard_map/pallas_call | solution.py:358
  45.4 1.4 %copy.21 = f32[4,2048]{1,0:T(4,128)} copy(f32[4,2048]{1,0:T(4,128)} %get-tuple-element.4) | data formatting | bytes 65536
  46.8 1.3 %copy.22 = f32[4,1024]{1,0:T(4,128)} copy(f32[4,1024]{1,0:T(4,128)} %get-tuple-element.5) | data formatting | bytes 32768

commit v3 on v2

--- a/solution.py
+++ b/solution.py
@@ -54,7 +54,7 @@
     q, nkv, kbuf, vbuf, wo, hid, g1, rt1, id1, gu1, dn1, tp, g2, rt2, id2, gu2, dn2,
     q_stage, o_stage, l_stage, att_send, att_recv, att_stage,
     terms, state_all, xn1, inner1, rep1, got1, part1, talk_all, xn2, inner2, rep2, got2, part2,
-    load_sem, kv_sem, send_sem, recv_sem,
+    load_sem, send_sem, recv_sem,
 ):
     s_me = lax.axis_index("seq")
     e_me = lax.axis_index("exp")
@@ -77,16 +77,121 @@
 
     load("q", q_hbm, q)
     load("nkv", nkv_hbm, nkv)
-    kv_loads = []
-    for c in range(count):
-        pair = [
-            pltpu.make_async_copy(kv_hbm.at[0, c], kbuf.at[c], kv_sem.at[2 * c]),
-            pltpu.make_async_copy(kv_hbm.at[1, c], vbuf.at[c], kv_sem.at[2 * c + 1]),
+    load("keys", kv_hbm.at[0], kbuf)
+    load("values", kv_hbm.at[1], vbuf)
+
+    barrier = pltpu.get_barrier_semaphore()
+
+    def along_seq(k):
+        return (lax.rem(s_me + k, nseq), e_me)
+
+    def along_exp(k):
+        to, bit = e_me, 1
+        while bit < nexp:
+            if (nexp - k) & bit:
+                to = to + bit * (1 - 2 * lax.rem(e_me // bit, 2))
+            bit = 2 * bit
+        return (s_me, to)
+
+    partners = [along_seq(k) for k in range(1, nseq)] + [along_exp(k) for k in range(1, nexp)]
+    for dev in partners:
+        pl.semaphore_signal(barrier, inc=1, device_id=dev, device_id_type=MESH)
+
+    def remote(src, dst, phase, dev):
+        return pltpu.make_async_remote_copy(
+            src_ref=src,
+            dst_ref=dst,
+            send_sem=send_sem.at[phase],
+            recv_sem=recv_sem.at[phase],
+            device_id=dev,
+            device_id_type=MESH,
+        )
+
+    def await_bytes(ref, sem):
+        pltpu.make_async_copy(ref, ref, sem).wait()
+
+    def gather(buf, phase, me_at, along, ways):
+        for k in range(1, ways):
+            remote(buf.at[me_at], buf.at[me_at], phase, along(k)).start()
+        await_bytes(buf.at[pl.ds(0, ways - 1)], recv_sem.at[phase])
+
+    def scatter(src, dst, phase, me_at, along, ways, axis):
+        for k in range(1, ways):
+            dev = along(k)
+            remote(src.at[dev[axis]], dst.at[me_at], phase, dev).start()
+        dst[me_at] = src[me_at]
+        await_bytes(dst.at[pl.ds(0, ways - 1)], recv_sem.at[phase])
+
+    def pack(x):
+        return [
+            jnp.concatenate(
+                [x[:, (i * stack + k) * 128 : (i * stack + k + 1) * 128] for k in range(stack)], axis=0
+            ).astype(BF16)
+            for i in range(x.shape[1] // (128 * stack))
         ]
-        for copy in pair:
-            copy.start()
-        kv_loads.append(pair)
+
+    def unpack(tiles):
+        return jnp.concatenate(
+            [t[k * count : (k + 1) * count] for t in tiles for k in range(stack)], axis=1
+        )
+
+    def summed(buf, ways):
+        return [
+            functools.reduce(jnp.add, [buf[w, i].astype(F32) for w in range(ways)])
+            for i in range(buf.shape[1])
+        ]
+
+    def all_rows(buf, out):
+        for i in range(buf.shape[1]):
+            tiles = [buf[e, i].astype(F32) for e in range(nexp)]
+            for k in range(stack):
+                at = (i * stack + k) * 128
+                out[:, at : at + 128] = jnp.concatenate(
+                    [t[k * count : (k + 1) * count] for t in tiles], axis=0
+                ).astype(BF16)
+
+    loads["q"].wait()
+    loads["nkv"].wait()
+    queries = q[...].astype(F32)
+    for h in range(H):
+        q_stage[h * 8 : h * 8 + count, :] = queries[:, h * HD : (h + 1) * HD]
+    groups = H // KVH
+    head_group = lax.broadcasted_iota(jnp.int32, (H, HD), 0) // groups
+    places = s_me * span + lax.broadcasted_iota(jnp.int32, (1, span), 1)
+    owner = s_me == 0
+    scale = HD ** (-0.5)
+    every = range(count)
+    spread = []
+    for c in every:
+        q_c = q_stage[pl.ds(c, H, stride=8), :]
+        spread.append(
+            jnp.concatenate([jnp.where(head_group == g, q_c, 0.0) for g in range(KVH)], axis=1)
+        )
+    fresh = [
+        jnp.sum(spread[c] * nkv[0, c : c + 1, :].astype(F32), axis=1, keepdims=True) * scale
+        for c in every
+    ]
+    fresh = [jnp.where(owner, x, -1e30) for x in fresh]
+    valid = [places < len_ref[c] for c in every]
+    loads["keys"].wait()
     load("wo", wo_hbm, wo)
+    scores = [
+        lax.dot_general(
+            spread[c].astype(BF16), kbuf[c], (((1,), (1,)), ((), ())), preferred_element_type=F32
+        )
+        * scale
+        for c in every
+    ]
+    masked = [jnp.where(valid[c], scores[c], -1e30) for c in every]
+    peak = [jnp.maximum(jnp.max(masked[c], axis=1, keepdims=True), fresh[c]) for c in every]
+    weights = [
+        jnp.where(valid[c], jnp.exp(masked[c] - peak[c]), 0.0).astype(BF16) for c in every
+    ]
+    fresh_weight = [jnp.where(owner, jnp.exp(fresh[c] - peak[c]), 0.0) for c in every]
+    total = [
+        jnp.sum(weights[c].astype(F32), axis=1, keepdims=True) + fresh_weight[c] for c in every
+    ]
+    loads["values"].wait()
     load("hid", hid_hbm, hid)
     load("g1", g1_hbm, g1)
     load("rt1", rt1_hbm, rt1)
@@ -99,112 +204,15 @@
     load("id2", id2_hbm, id2)
     load("gu2", gu2_hbm.at[0], gu2)
     load("dn2", dn2_hbm.at[0], dn2)
-
-    barrier = pltpu.get_barrier_semaphore()
-
-    def along_seq(k):
-        return (lax.rem(s_me + k, nseq), e_me)
-
-    def along_exp(k):
-        return (s_me, lax.rem(e_me + k, nexp))
-
-    partners = [along_seq(k) for k in range(1, nseq)] + [along_exp(k) for k in range(1, nexp)]
-    for dev in partners:
-        pl.semaphore_signal(barrier, inc=1, device_id=dev, device_id_type=MESH)
-
-    def remote(src, dst, phase, dev):
-        return pltpu.make_async_remote_copy(
-            src_ref=src,
-            dst_ref=dst,
-            send_sem=send_sem.at[phase],
-            recv_sem=recv_sem.at[phase],
-            device_id=dev,
-            device_id_type=MESH,
-        )
-
-    def await_bytes(ref, sem):
-        pltpu.make_async_copy(ref, ref, sem).wait()
-
-    def gather(buf, phase, me_at, along, ways):
-        for k in range(1, ways):
-            remote(buf.at[me_at], buf.at[me_at], phase, along(k)).start()
-        await_bytes(buf.at[pl.ds(0, ways - 1)], recv_sem.at[phase])
-
-    def scatter(src, dst, phase, me_at, along, ways, axis):
-        for k in range(1, ways):
-            dev = along(k)
-            remote(src.at[dev[axis]], dst.at[me_at], phase, dev).start()
-        dst[me_at] = src[me_at]
-        await_bytes(dst.at[pl.ds(0, ways - 1)], recv_sem.at[phase])
-
-    def pack(x):
-        return [
-            jnp.concatenate(
-                [x[:, (i * stack + k) * 128 : (i * stack + k + 1) * 128] for k in range(stack)], axis=0
-            ).astype(BF16)
-            for i in range(x.shape[1] // (128 * stack))
-        ]
-
-    def unpack(tiles):
-        return jnp.concatenate(
-            [t[k * count : (k + 1) * count] for t in tiles for k in range(stack)], axis=1
-        )
-
-    def summed(buf, ways):
-        return [
-            functools.reduce(jnp.add, [buf[w, i].astype(F32) for w in range(ways)])
-            for i in range(buf.shape[1])
-        ]
-
-    def all_rows(buf, out):
-        for i in range(buf.shape[1]):
-            tiles = [buf[e, i].astype(F32) for e in range(nexp)]
-            for k in range(stack):
-                at = (i * stack + k) * 128
-                out[:, at : at + 128] = jnp.concatenate(
-                    [t[k * count : (k + 1) * count] for t in tiles], axis=0
-                ).astype(BF16)
-
-    loads["q"].wait()
-    loads["nkv"].wait()
-    queries = q[...].astype(F32)
-    for h in range(H):
-        q_stage[h * 8 : h * 8 + count, :] = queries[:, h * HD : (h + 1) * HD]
-    groups = H // KVH
-    head_group = lax.broadcasted_iota(jnp.int32, (H, HD), 0) // groups
-    places = s_me * span + lax.broadcasted_iota(jnp.int32, (1, span), 1)
-    owner = s_me == 0
-    scale = HD ** (-0.5)
-    for c in range(count):
-        q_c = q_stage[pl.ds(c, H, stride=8), :]
-        spread = jnp.concatenate(
-            [jnp.where(head_group == g, q_c, 0.0) for g in range(KVH)], axis=1
-        )
-        new_k = nkv[0, c : c + 1, :].astype(F32)
-        new_v = nkv[1, c : c + 1, :].astype(F32)
-        kv_loads[c][0].wait()
-        scores = lax.dot_general(
-            spread.astype(BF16), kbuf[c], (((1,), (1,)), ((), ())), preferred_element_type=F32
-        ) * scale
-        fresh = jnp.sum(spread * new_k, axis=1, keepdims=True) * scale
-        fresh = jnp.where(owner, fresh, -1e30)
-        valid = places < len_ref[c]
-        masked = jnp.where(valid, scores, -1e30)
-        peak = jnp.maximum(jnp.max(masked, axis=1, keepdims=True), fresh)
-        weights = jnp.where(valid, jnp.exp(masked - peak), 0.0).astype(BF16)
-        fresh_weight = jnp.where(owner, jnp.exp(fresh - peak), 0.0)
-        total = jnp.sum(weights.astype(F32), axis=1, keepdims=True) + fresh_weight
-        kv_loads[c][1].wait()
-        mixed = jnp.dot(weights, vbuf[c], preferred_element_type=F32) + fresh_weight * new_v
-        some = total > 0.0
-        safe = jnp.where(some, total, 1.0)
-        lse = jnp.where(some, peak + jnp.log(safe), -1e30)
-        inverse = 1.0 / safe
-        mixed = mixed * inverse
-        lse = jnp.broadcast_to(lse, (H, HD))
-        own = mixed[:, 0:HD]
+    mixed = [jnp.dot(weights[c], vbuf[c], preferred_element_type=F32) for c in every]
+    for c in every:
+        some = total[c] > 0.0
+        safe = jnp.where(some, total[c], 1.0)
+        lse = jnp.broadcast_to(jnp.where(some, peak[c] + jnp.log(safe), -1e30), (H, HD))
+        whole = (mixed[c] + fresh_weight[c] * nkv[1, c : c + 1, :].astype(F32)) * (1.0 / safe)
+        own = whole[:, 0:HD]
         for g in range(1, KVH):
-            own = jnp.where(head_group == g, mixed[:, g * HD : (g + 1) * HD], own)
+            own = jnp.where(head_group == g, whole[:, g * HD : (g + 1) * HD], own)
         for t in range(nseq):
             o_stage[t, c * hp : (c + 1) * hp, :] = own[t * hp : (t + 1) * hp]
             l_stage[t, c * hp : (c + 1) * hp, :] = lse[t * hp : (t + 1) * hp]
@@ -350,8 +358,7 @@
         pltpu.VMEM((rows, dt), BF16), pltpu.VMEM((rows, ft), BF16),
         pltpu.VMEM((nexp, dt // wide, RB, 128), BF16), pltpu.VMEM((nexp, dt // wide, RB, 128), BF16),
         pltpu.VMEM((nseq, dt // wide, RB, 128), BF16),
-        pltpu.SemaphoreType.DMA((16,)),
-        pltpu.SemaphoreType.DMA((2 * count,)),
+        pltpu.SemaphoreType.DMA((17,)),
         pltpu.SemaphoreType.DMA((8,)),
         pltpu.SemaphoreType.DMA((8,)),
     ]

time: 48.3 us -> 43.3 us (0.90)
  Pallas kernels: 44.7 us -> 39.7 us
    pallas_call x1, Pallas kernels: 44.7 us -> 39.7 us  [on_device(): pl.pallas_call(functools.partial(kernel, nseq, nexp), out_shape=(jax.Shap...]
where the time goes in v3:
time: 43.3 us; the launch traced here: 43 us
  Pallas kernels  39.7 us (92%)
  local copies, waits for them, and re-layouts  2.7 us (6%)
  between operations  0.65 us (2%)
    pallas_call x1, Pallas kernels, on_device(): pl.pallas_call(functools.partial(kernel, nseq, nexp), out_shape=(jax.Shap...  39.7 us
    unnamed x2, local copies, waits for them, and re-layouts  2.7 us

profile of v3, /device:TPU:0, one launch (start us, length us, event | category | flops | bytes accessed | tf_op | source)
XLA Modules:
  0.0 43.0 jit_solution(59186445240601962)
XLA Ops:
  0.6 39.7 %shard_map.176 = (f32[4,2048]{1,0:T(4,128)}, f32[4,1024]{1,0:T(4,128)}) custom-call(bf16[4,4096]{1,0:T(4,128)(2,1)} %q_hbm.1, bf16[2,4,512]{2,1,0:T(4,128)(2,1)} %nkv_hbm.1, bf16[2,4,512,512]{3,2,1,0:T(8,128)(2,1)} %kv_hbm.1, s32[4]{0:T(128)} %len_ref.1, bf16[1024,2048]{1,0:T(8,128)(2,1)} %wo_hbm.1, f32[4,2048]{1,0:T(4,128)} %hid_hbm.1, f32[1,2048]{1,0:T(1,128)} %bitcast.8, ...), custom_call_target="tpu_custom_call" | custom-call | tf_op jit(solution)/shard_map/pallas_call | solution.py:365
  40.3 1.4 %copy.21 = f32[4,2048]{1,0:T(4,128)} copy(f32[4,2048]{1,0:T(4,128)} %get-tuple-element.4) | data formatting | bytes 65536
  41.7 1.3 %copy.22 = f32[4,1024]{1,0:T(4,128)} copy(f32[4,1024]{1,0:T(4,128)} %get-tuple-element.5) | data formatting | bytes 32768

commit v4 on v3

--- a/solution.py
+++ b/solution.py
@@ -248,15 +248,20 @@
 
     loads["wo"].wait()
     wide = 128 * stack
+    half = d // wide // 2
     for i in range(d // wide):
         term = jnp.dot(heads, wo[:, i * wide : (i + 1) * wide], preferred_element_type=F32)
         terms[s_me, i] = pack(term)[0]
-    gather(terms, 1, s_me, along_seq, nseq)
+        if (i + 1) % half == 0:
+            for k in range(1, nseq):
+                own = terms.at[s_me, pl.ds(i + 1 - half, half)]
+                remote(own, own, 1, along_seq(k)).start()
+    await_bytes(terms.at[pl.ds(0, nseq - 1)], recv_sem.at[1])
     loads["hid"].wait()
     loads["g1"].wait()
     state = hid[...] + unpack(summed(terms, nseq))
 
-    def experts(xn, router, ids, gu, dn, inner, rep, width, hidden):
+    def experts(xn, router, ids, gu, dn, inner, rep, got, phase, width, hidden):
         gate = own_gate(xn, router, ids, me)
         step = 256 if hidden % 256 == 0 else 128
         for i in range(hidden // step):
@@ -268,6 +273,13 @@
             y = jnp.where(gate > 0.0, gate * y, 0.0)
             for e in range(nexp):
                 rep[e, i] = pack(y[e * count : (e + 1) * count])[0]
+            if (i + 1) % 2 == 0:
+                for k in range(1, nexp):
+                    dev = along_exp(k)
+                    piece = pl.ds(i - 1, 2)
+                    remote(rep.at[dev[1], piece], got.at[e_me, piece], phase, dev).start()
+        got[e_me] = rep[e_me]
+        await_bytes(got.at[pl.ds(0, nexp - 1)], recv_sem.at[phase])
 
     def layer(stream, gain, everyone, xn, router, ids, gu, dn, inner, rep, got, part, phase, names):
         for i, tile in enumerate(pack(normalise(stream, gain).astype(F32))):
@@ -276,8 +288,7 @@
         all_rows(everyone, xn)
         for name in names:
             loads[name].wait()
-        experts(xn, router, ids, gu, dn, inner, rep, stream.shape[1], inner.shape[1])
-        scatter(rep, got, phase + 1, e_me, along_exp, nexp, 1)
+        experts(xn, router, ids, gu, dn, inner, rep, got, phase + 1, stream.shape[1], inner.shape[1])
         for i, tile in enumerate(summed(got, nexp)):
             part[s_me, i] = tile.astype(BF16)
         gather(part, phase + 2, s_me, along_seq, nseq)
@@ -314,6 +325,15 @@
         (7, part2, nseq),
     ):
         await_bytes(buf.at[pl.ds(0, ways - 1)], send_sem.at[phase])
+
+
+def hand_over(from1, from2, to1, to2, sem):
+    first = pltpu.make_async_copy(from1, to1, sem.at[0])
+    second = pltpu.make_async_copy(from2, to2, sem.at[1])
+    first.start()
+    second.start()
+    first.wait()
+    second.wait()
 
 
 def on_device(
@@ -362,12 +382,13 @@
         pltpu.SemaphoreType.DMA((8,)),
         pltpu.SemaphoreType.DMA((8,)),
     ]
-    return pl.pallas_call(
+    outs = (
+        jax.ShapeDtypeStruct((count, d), F32),
+        jax.ShapeDtypeStruct((count, dt), F32),
+    )
+    both = pl.pallas_call(
         functools.partial(kernel, nseq, nexp),
-        out_shape=(
-            jax.ShapeDtypeStruct((count, d), F32),
-            jax.ShapeDtypeStruct((count, dt), F32),
-        ),
+        out_shape=outs,
         in_specs=in_specs,
         out_specs=(vmem_spec, vmem_spec),
         scratch_shapes=scratch,
@@ -375,6 +396,14 @@
             collective_id=0, has_side_effects=True, vmem_limit_bytes=56 * 1024 * 1024
         ),
     )(*args)
+    return pl.pallas_call(
+        hand_over,
+        out_shape=outs,
+        in_specs=[any_spec] * 2,
+        out_specs=(any_spec, any_spec),
+        scratch_shapes=[pltpu.SemaphoreType.DMA((2,))],
+        compiler_params=pltpu.CompilerParams(vmem_limit_bytes=60 * 1024 * 1024),
+    )(*both)
 
 
 def solution(mesh):

time: 43.3 us -> 42.9 us (level)
  local copies, waits for them, and re-layouts: 2.7 us -> 0 us
  Pallas kernels: 39.7 us -> 42.1 us
    unnamed x2 -> x0, local copies, waits for them, and re-layouts: 2.7 us -> none
    pallas_call x1 -> x2, Pallas kernels: 39.7 us -> 42.1 us  [the longest x1 39.5 us: on_device(): pl.pallas_call(functools.partial(kernel, nseq, nexp), out_shape=outs, in_...]
where the time goes in v4:
time: 42.9 us; the launch traced here: 42.7 us
  Pallas kernels  42.1 us (98%)
  between operations  0.65 us (2%)
    pallas_call x1, Pallas kernels, on_device(): pl.pallas_call(functools.partial(kernel, nseq, nexp), out_shape=outs, in_...  39.5 us
    pallas_call x1, Pallas kernels, on_device(): pl.pallas_call(hand_over, out_shape=outs, in_specs=[any_spec] * 2, out_sp...  2.61 us

profile of v4, /device:TPU:0, one launch (start us, length us, event | category | flops | bytes accessed | tf_op | source)
XLA Modules:
  0.0 42.7 jit_solution(572725891198454846)
XLA Ops:
  0.6 39.5 %shard_map.176 = (f32[4,2048]{1,0:T(4,128)}, f32[4,1024]{1,0:T(4,128)}) custom-call(bf16[4,4096]{1,0:T(4,128)(2,1)} %q_hbm.1, bf16[2,4,512]{2,1,0:T(4,128)(2,1)} %nkv_hbm.1, bf16[2,4,512,512]{3,2,1,0:T(8,128)(2,1)} %kv_hbm.1, s32[4]{0:T(128)} %len_ref.1, bf16[1024,2048]{1,0:T(8,128)(2,1)} %wo_hbm.1, f32[4,2048]{1,0:T(4,128)} %hid_hbm.1, f32[1,2048]{1,0:T(1,128)} %bitcast.8, ...), custom_call_target="tpu_custom_call" | custom-call | tf_op jit(solution)/shard_map/pallas_call | solution.py:389
  40.1 2.6 %shard_map.177 = (f32[4,2048]{1,0:T(4,128)}, f32[4,1024]{1,0:T(4,128)}) custom-call(f32[4,2048]{1,0:T(4,128)} %get-tuple-element.4.from1, f32[4,1024]{1,0:T(4,128)} %get-tuple-element.5.from2), custom_call_target="tpu_custom_call" | custom-call | tf_op jit(solution)/shard_map/pallas_call | solution.py:399
